TPU v7x, 128 devices: a whole 4x4x4 slice. The times are simulated.
128 devices in a mesh: row: 4 (over x_hi, core), pair: 32 (over y, z, x_lo).
Axes of the slice: x: 4 (x_hi: 2, x_lo: 2; x = x_hi * 2 + x_lo), y: 4, z: 4, core: 2. Of those that a mesh axis runs over, the one named last changes fastest.
Arguments:
- samples: bfloat16 [32768, 16384], P(('row', 'pair')), may hold values from -6 to 6
Outputs:
- rotated: bfloat16 [32768, 16384], P('row', 'pair')
All inputs are finite; a program needn't handle non-finite values.
Results may differ from a plain program's by a relative error of at most 0.0046.
Values may be sent and summed in bfloat16 or wider, within the bound.
A program may use at most 128 MiB of HBM per device.

v0:
```python
import jax
import jax.numpy as jnp
from jax import lax
from jax.sharding import PartitionSpec as P

NS_STEPS = 5


def shifted(shard, axis, by):
    peers = lax.axis_size(axis)
    return lax.ppermute(shard, axis, [(i, (i + by) % peers) for i in range(peers)])


def newton_steps(scaled):
    width = scaled.shape[0]
    eye_mat = jnp.eye(width, dtype=jnp.float32)
    matrix_m = scaled
    inverse_z = eye_mat
    for step in range(NS_STEPS):
        factor_s = 1.5 * eye_mat - 0.5 * jnp.dot(
            inverse_z, matrix_m, precision=lax.Precision.HIGHEST
        )
        matrix_m = jnp.dot(matrix_m, factor_s, precision=lax.Precision.HIGHEST)
        inverse_z = jnp.dot(factor_s, inverse_z, precision=lax.Precision.HIGHEST)
    return inverse_z


def cross_product(first, second):
    return lax.dot_general(
        first, second, (((0,), (0,)), ((), ())), preferred_element_type=jnp.float32
    )


def body(samples):
    relaid = lax.all_to_all(samples, "pair", split_axis=1, concat_axis=0, tiled=True)
    column_count = relaid.shape[1]
    middle = column_count // 2
    gram_matrix = lax.psum(cross_product(relaid, relaid), "row")
    rows_total = relaid.shape[0] * lax.axis_size("row")
    frobenius = jnp.sqrt(jnp.sum(gram_matrix * gram_matrix))
    inverse_z = newton_steps(gram_matrix / frobenius)
    rotation = (inverse_z * jnp.sqrt(rows_total / frobenius)).astype(jnp.bfloat16)
    turned = jnp.dot(relaid, rotation, preferred_element_type=jnp.float32).astype(jnp.bfloat16)
    moved = shifted(turned[:, middle:], "pair", 1)
    return jnp.concatenate([turned[:, :middle], moved], axis=1)


def solution(mesh):
    placed = (P(("row", "pair"), None),)
    return jax.shard_map(
        body, mesh=mesh, in_specs=placed, out_specs=P("row", "pair"), check_vma=False
    )
```

profile of v0, /device:TPU:1, one launch (start us, length us, event | category | flops | bytes accessed | tf_op | source)
XLA Modules:
  0.0 359.4 jit_solution(141522543583162237)
XLA Ops:
  6.5 0.0 all-reduce.2.cloned.1.call-start
  6.5 11.9 %copy.4 = bf16[256,16384]{0,1:T(8,128)(2,1)} copy(bf16[256,16384]{1,0:T(8,128)(2,1)} %param.1) | data formatting | bytes 16777216 | tf_op args[0]
  18.4 12.0 %copy.5 = bf16[256,32,512]{2,0,1:T(8,128)(2,1)} copy(bf16[256,32,512]{0,2,1:T(8,128)(2,1)} %bitcast.38) | data formatting | bytes 16777216 | tf_op jit(solution)/shard_map/all_to_all | solution.py:35
  30.4 105.7 %all_to_all.19 = bf16[256,32,512]{2,0,1:T(8,128)(2,1)S(1)} all-to-all(bf16[256,32,512]{2,0,1:T(8,128)(2,1)} %copy.5), channel_id=1, replica_groups=mesh['row'=4,'pair'=32] {'pair'}, dimensions={1} | all-to-all | bytes 16777216 | tf_op jit(solution)/shard_map/all_to_all | solution.py:35
  136.2 0.0 copy-start
  136.2 3.4 copy-done
  139.6 5.5 %fusion.3 = f32[512,512]{1,0:T(8,128)} fusion(bf16[256,32,512]{2,0,1:T(8,128)(2,1)S(1)} %all_to_all.19), kind=kOutput, calls=%fused_computation.10 | convolution fusion | flops 4294967296 | bytes 9437184 | tf_op jit(solution)/shard_map/dot_general | solution.py:29
  145.1 0.0 all-reduce.2.cloned.1.call-update
  145.1 45.1 %all-reduce.2.cloned.1.call-done = f32[512,512]{1,0:T(8,128)} async-done(((f32[512,512]{1,0:T(8,128)}), f32[512,512]{1,0:T(8,128)}) %all-reduce.2.cloned.1.call-update) | async-done | bytes 1048592 | tf_op jit(solution)/shard_map/psum | solution.py:38
  190.2 0.0 copy-start.2
  190.2 2.3 multiply_reduce_fusion
  193.2 2.3 select_subtract_fusion.4
  195.5 1.0 fusion.7
  196.5 0.0 copy-done.2
  196.5 1.9 fusion.8
  198.4 1.9 select_subtract_fusion.3
  200.2 1.8 fusion.11
  202.1 2.0 fusion.10
  204.1 1.9 select_subtract_fusion.2
  206.0 1.8 fusion.13
  207.8 1.8 fusion.12
  209.7 1.8 select_subtract_fusion.1
  211.5 1.8 fusion.14
  213.4 1.8 fusion.15
  215.3 2.1 select_subtract_fusion
  217.4 1.9 fusion.6
  219.3 10.2 %fusion = bf16[8192,512]{0,1:T(8,128)(2,1)} fusion(bf16[512,512]{1,0:T(8,128)(2,1)S(1)} %fusion.6, bf16[8192,512]{1,0:T(8,128)(2,1)} %bitcast.39), kind=kOutput, calls=%fused_computation.1 | convolution fusion | flops 4299161600 | bytes 17301504 | tf_op jit(solution)/shard_map/dot_general | solution.py:43
  229.5 5.2 %fusion.9 = (bf16[8192,256]{0,1:T(8,128)(2,1)}, bf16[8192,256]{0,1:T(8,128)(2,1)S(1)}) fusion(bf16[8192,512]{0,1:T(8,128)(2,1)} %fusion), kind=kLoop, calls=%fused_computation.23 | loop fusion | bytes 16777216 | tf_op jit(solution)/shard_map/slice | solution.py:45
  234.7 0.3 collective-permute-start
  235.0 96.0 %collective-permute-done = bf16[8192,256]{0,1:T(8,128)(2,1)S(1)} collective-permute-done((bf16[8192,256]{0,1:T(8,128)(2,1)S(1)}, bf16[8192,256]{0,1:T(8,128)(2,1)S(1)}, u32[]{:S(2)}, u32[]{:S(2)}) %collective-permute-start) | collective-permute-done | bytes 4194336 | tf_op jit(solution)/shard_map/ppermute | solution.py:11
  331.0 0.0 copy-start.1
  331.0 2.0 copy-done.1
  332.9 7.7 %pad_maximum_fusion = bf16[8192,512]{0,1:T(8,128)(2,1)} fusion(bf16[8192,256]{0,1:T(8,128)(2,1)} %copy-done.1, bf16[8192,256]{0,1:T(8,128)(2,1)} %get-tuple-element.5), kind=kLoop, calls=%fused_computation.2 | loop fusion | flops 16777216 | bytes 16777216 | tf_op jit(solution)/shard_map/concatenate | solution.py:45
  340.6 11.9 %copy.7 = bf16[8192,512]{1,0:T(8,128)(2,1)} copy(bf16[8192,512]{0,1:T(8,128)(2,1)} %pad_maximum_fusion) | data formatting | bytes 16777216 | tf_op jit(solution)/shard_map/concatenate | solution.py:45
Async XLA Ops:
  6.5 183.7 %all-reduce.2.cloned.1.call-start = ((), (), s32[]{:S(2)}) async-start(), calls=%async_computation.1 | async-start | bytes 2097152 | tf_op jit(solution)/shard_map/psum | solution.py:38
  136.2 3.4 copy-start
  190.2 6.2 %copy-start.2 = (f32[512,512]{1,0:T(8,128)S(1)}, f32[512,512]{1,0:T(8,128)}, u32[]{:S(2)}) copy-start(f32[512,512]{1,0:T(8,128)} %all-reduce.2.cloned.1.call-done) | copy-start | bytes 3145732
  234.7 96.2 %collective-permute-start = (bf16[8192,256]{0,1:T(8,128)(2,1)S(1)}, bf16[8192,256]{0,1:T(8,128)(2,1)S(1)}, u32[]{:S(2)}, u32[]{:S(2)}) collective-permute-start(bf16[8192,256]{0,1:T(8,128)(2,1)S(1)} %get-tuple-element.6), channel_id=1, source_target_pairs={{0,1},{1,2},{2,3},{3,4},{4,5},{5,6},{6,7},{7,8},{8,9},{9,10},{10,1... | collective-permute-start | bytes 12582920 | tf_op jit(solution)/shard_map/ppermute | solution.py:11
  331.0 2.0 copy-start.1
Sparse Core Ops, SparseCore 0:
  145.2 44.9 all-reduce.1
where the time goes:
time: 360 us; the launch traced here: 359 us
  waiting for transfers between devices  141 us (39%)
  blocking collectives  106 us (29%)
  local copies, waits for them, and re-layouts  46.4 us (13%)
  matrix products  41.7 us (12%)
  between operations  14.3 us (4%)
  other arithmetic  9.94 us (3%)
    all_to_all x1, blocking collectives, body(): lax.all_to_all(samples, 'pair', split_axis=1, concat_axis=0, tiled=True)  106 us
    ppermute x1, waiting for transfers between devices, shifted(): lax.ppermute(shard, axis, [(i, (i + by) % peers) for i in range(peers)])  96 us
    psum x1, waiting for transfers between devices, body(): gram_matrix = lax.psum(cross_product(relaid, relaid), 'row')  45.1 us
    unnamed x7, local copies, waits for them, and re-layouts  17.3 us
    all_to_all x1, local copies, waits for them, and re-layouts, body(): lax.all_to_all(samples, 'pair', split_axis=1, concat_axis=0, tiled=True)  12 us
    concatenate x1, local copies, waits for them, and re-layouts, body(): return jnp.concatenate([turned[:, :middle], moved], axis=1)  11.9 us
    dot_general x1, matrix products, body(): jnp.dot(relaid, rotation, preferred_element_type=jnp.float32)  10.2 us
    dot_general x5, matrix products, newton_steps(): jnp.dot(inverse_z, matrix_m, precision=lax.Precision.HIGHEST)  9.95 us
  transfers between devices with their start and end apart: 2, of which 2 were waited for; matrix products, arithmetic and copies ran while one was open for 0% of the time, Pallas kernels for 0%

commit v1 on v0

v1 whole, which is shorter than its diff:
```python
import functools

import jax
import jax.numpy as jnp
from jax import lax
from jax.experimental import pallas as pl
from jax.experimental.pallas import tpu as pltpu
from jax.sharding import PartitionSpec as P

MESH = pl.DeviceIdType.MESH
F32 = jnp.float32
BF16 = jnp.bfloat16
NS_STEPS = 5
ROWS = 32768
CHIPS = 16
PEERS = CHIPS - 1
SUBS = 4
CHUNK = 64
PAIR = 512
HALF = 256
PACKED = 3 * HALF
CORE_PART = PACKED // 2
QUARTER = CORE_PART // 4
SENDS = 2 * SUBS * PEERS


def dot(left, right, dims=((1,), (0,))):
    return lax.dot_general(left, right, (dims, ((), ())), preferred_element_type=F32)


def split(ref_hi, ref_lo, value):
    high = value.astype(BF16)
    ref_hi[...] = high
    ref_lo[...] = (value - high.astype(F32)).astype(BF16)


def product(left, right):
    lh, ll = left
    rh, rl = right
    return dot(lh[...], rh[...]) + (dot(lh[...], rl[...]) + dot(ll[...], rh[...]))


def kernel(
    x_ref, o_ref,
    y, part, from_core, from_quarter, full, zmat, mmat, zh, zl, mh, ml, th, tl, rot, w_send, w_keep,
    own_sem, a2a_send, a2a_recv, core_send, core_recv, rs_send, rs_recv, ag_send, ag_recv,
    back_send, back_recv, w_send_sem, w_recv_sem, w_keep_sem,
):
    row = lax.axis_index("row")
    pair = lax.axis_index("pair")
    core = lax.rem(row, 2)
    x_hi = row // 2
    plane = lax.rem(pair, 2)
    chip = pair // 2
    y_pos, z_pos = chip // 4, lax.rem(chip, 4)
    quarter = x_hi * 2 + plane

    def member(stage, step):
        other = lax.rem(quarter + step, 4)
        other_plane = lax.rem(other, 2)
        other_chip = chip
        if stage == 1:
            other_chip = lax.rem(chip + plane - other_plane + CHIPS, CHIPS)
        return other, ((other // 2) * 2 + core, other_chip * 2 + other_plane)

    core_peer = (x_hi * 2 + 1 - core, pair)

    def partner(stage):
        other_chip = chip
        if stage == 1:
            other_chip = lax.rem(chip + 2 * plane - 1 + CHIPS, CHIPS)
        return (row, other_chip * 2 + 1 - plane)

    barrier = pltpu.get_barrier_semaphore()

    def greet(device):
        pl.semaphore_signal(barrier, inc=1, device_id=device, device_id_type=MESH)

    def offset(i):
        turn = 1 + lax.rem(i * 7, PEERS)
        return lax.rem(y_pos + turn // 4, 4) * 4 + lax.rem(z_pos + lax.rem(turn, 4), 4)

    def greet_plane(i, carry):
        greet((row, offset(i) * 2 + plane))
        return carry

    lax.fori_loop(0, PEERS, greet_plane, 0)
    greet(core_peer)
    for step in range(1, 4):
        greet(member(0, step)[1])
    greet(member(1, 1)[1])
    greet(member(1, 3)[1])

    def columns_of(stage, target):
        index = 2 * target
        if not isinstance(stage, int):
            index = index + stage * (2 * plane - 1)
        elif stage == 1:
            index = index + 2 * plane - 1
        index = lax.rem(index + 2 * CHIPS, 2 * CHIPS)
        return pl.ds(pl.multiple_of(index * PAIR, PAIR), PAIR)

    def own_copy(stage):
        return pltpu.make_async_copy(
            x_ref.at[:, :, columns_of(stage, chip)], y.at[stage, :, chip], own_sem.at[stage]
        )

    for stage in range(2):
        own_copy(stage).start()
    pl.semaphore_wait(barrier, PEERS + 6)

    def a2a_copy(n):
        phase, i = n // PEERS, lax.rem(n, PEERS)
        stage, sub = phase // SUBS, lax.rem(phase, SUBS)
        target = offset(i)
        return pltpu.make_async_remote_copy(
            src_ref=x_ref.at[sub, :, columns_of(stage, target)],
            dst_ref=y.at[stage, sub, chip],
            send_sem=a2a_send.at[i],
            recv_sem=a2a_recv.at[phase],
            device_id=(row, target * 2 + plane),
            device_id_type=MESH,
        )

    def a2a_first(n, carry):
        a2a_copy(n).start()
        return carry

    def a2a_next(n, carry):
        a2a_copy(n - PEERS).wait_send()
        a2a_copy(n).start()
        return carry

    sent = [0]

    def pump(count):
        stop = min(SENDS, sent[0] + count)
        if stop > sent[0]:
            lax.fori_loop(sent[0], stop, a2a_next, 0)
            sent[0] = stop

    def a2a_arrived(stage, sub):
        landed = y.at[stage, sub, pl.ds(0, PEERS)]
        pltpu.make_async_copy(landed, landed, a2a_recv.at[stage * SUBS + sub]).wait()

    def gram(stage, sub):
        rows = y[stage, sub].reshape(CHIPS * CHUNK, PAIR)
        left, right = rows[:, :HALF], rows[:, HALF:]
        for index, (one, two) in enumerate(((left, left), (left, right), (right, right))):
            here = pl.ds(index * HALF, HALF)
            term = dot(one, two, ((0,), (0,)))
            if sub == 0:
                part[stage, here] = term
            else:
                part[stage, here] += term

    core_rows = pl.ds(pl.multiple_of(core * CORE_PART, CORE_PART), CORE_PART)
    peer_rows = pl.ds(pl.multiple_of((1 - core) * CORE_PART, CORE_PART), CORE_PART)

    def quarter_rows(which):
        return pl.ds(pl.multiple_of(core * CORE_PART + which * QUARTER, QUARTER), QUARTER)

    def core_copy(stage):
        return pltpu.make_async_remote_copy(
            src_ref=part.at[stage, peer_rows], dst_ref=from_core.at[stage],
            send_sem=core_send.at[stage], recv_sem=core_recv.at[stage],
            device_id=core_peer, device_id_type=MESH,
        )

    def rs_copy(stage, step):
        other, device = member(stage, step)
        return pltpu.make_async_remote_copy(
            src_ref=part.at[stage, quarter_rows(other)], dst_ref=from_quarter.at[stage, step - 1],
            send_sem=rs_send.at[stage, step - 1], recv_sem=rs_recv.at[stage, step - 1],
            device_id=device, device_id_type=MESH,
        )

    def ag_copy(stage, step):
        _, device = member(stage, step)
        return pltpu.make_async_remote_copy(
            src_ref=full.at[stage, quarter_rows(quarter)], dst_ref=full.at[stage, quarter_rows(quarter)],
            send_sem=ag_send.at[stage, step - 1], recv_sem=ag_recv.at[stage, step - 1],
            device_id=device, device_id_type=MESH,
        )

    def back_copy(stage):
        return pltpu.make_async_remote_copy(
            src_ref=full.at[stage, core_rows], dst_ref=full.at[stage, core_rows],
            send_sem=back_send.at[stage], recv_sem=back_recv.at[stage],
            device_id=core_peer, device_id_type=MESH,
        )

    def reduce_1(stage):
        core_copy(stage).start()

    def reduce_2(stage):
        core_copy(stage).wait_recv()
        part[stage, core_rows] += from_core[stage]
        for step in (2, 1, 3):
            rs_copy(stage, step).start()

    def reduce_3(stage):
        total = part[stage, quarter_rows(quarter)]
        for step in (1, 3, 2):
            rs_copy(stage, step).wait_recv()
            total = total + from_quarter[stage, step - 1]
        full[stage, quarter_rows(quarter)] = total
        for step in (2, 1, 3):
            ag_copy(stage, step).start()

    def reduce_4(stage):
        for step in (1, 3, 2):
            ag_copy(stage, step).wait_recv()
        back_copy(stage).start()

    def reduce_5(stage):
        back_copy(stage).wait_recv()
        for step in range(1, 4):
            rs_copy(stage, step).wait_send()
            ag_copy(stage, step).wait_send()
        core_copy(stage).wait_send()
        back_copy(stage).wait_send()

    diagonal = lambda: (
        lax.broadcasted_iota(jnp.int32, (PAIR, PAIR), 0) == lax.broadcasted_iota(jnp.int32, (PAIR, PAIR), 1)
    ).astype(F32)

    def newton(stage, between):
        g00 = full[stage, pl.ds(0, HALF)]
        g01 = full[stage, pl.ds(HALF, HALF)]
        g11 = full[stage, pl.ds(2 * HALF, HALF)]
        square = (
            jnp.sum(g00 * g00, keepdims=True) + 2.0 * jnp.sum(g01 * g01, keepdims=True)
            + jnp.sum(g11 * g11, keepdims=True)
        )
        norm = jnp.sqrt(square)
        mmat[:HALF, :HALF] = g00 / norm
        mmat[:HALF, HALF:] = g01 / norm
        mmat[HALF:, :HALF] = (g01 / norm).T
        mmat[HALF:, HALF:] = g11 / norm
        split(mh, ml, mmat[...])
        zmat[...] = 1.5 * diagonal() - 0.5 * mmat[...]
        mmat[...] = 1.5 * mmat[...] - 0.5 * product((mh, ml), (mh, ml))
        split(zh, zl, zmat[...])
        split(mh, ml, mmat[...])
        between()
        for _ in range(NS_STEPS - 2):
            split(th, tl, product((zh, zl), (mh, ml)))
            mmat[...] = 1.5 * mmat[...] - 0.5 * product((mh, ml), (th, tl))
            zmat[...] = 1.5 * zmat[...] - 0.5 * product((th, tl), (zh, zl))
            split(zh, zl, zmat[...])
            split(mh, ml, mmat[...])
            between()
        split(th, tl, product((zh, zl), (mh, ml)))
        last = 1.5 * zmat[...] - 0.5 * product((th, tl), (zh, zl))
        rot[stage] = (last * jnp.sqrt(ROWS / norm)).astype(BF16)

    def half_of(stage, kept):
        which = plane if (stage == 0) == kept else 1 - plane
        return pl.ds(pl.multiple_of(which * HALF, HALF), HALF)

    def send_copy(stage, sub):
        return pltpu.make_async_remote_copy(
            src_ref=w_send.at[stage, sub],
            dst_ref=o_ref.at[:, plane, sub, :, half_of(stage, False)],
            send_sem=w_send_sem.at[stage, sub], recv_sem=w_recv_sem.at[stage, sub],
            device_id=partner(stage), device_id_type=MESH,
        )

    def keep_copy(stage, sub):
        return pltpu.make_async_copy(
            w_keep.at[stage, sub],
            o_ref.at[:, plane, sub, :, half_of(stage, True)],
            w_keep_sem.at[stage, sub],
        )

    def apply(stage, sub, kept):
        rows = y[stage, sub].reshape(CHIPS * CHUNK, PAIR)
        value = dot(rows, rot[stage, :, half_of(stage, kept)]).astype(BF16)
        (w_keep if kept else w_send)[stage, sub] = value.reshape(CHIPS, CHUNK, HALF)
        (keep_copy if kept else send_copy)(stage, sub).start()

    lax.fori_loop(0, PEERS, a2a_first, 0)
    sent[0] = PEERS
    for sub in range(SUBS):
        pump(PEERS)
        if sub == 0:
            own_copy(0).wait()
        a2a_arrived(0, sub)
        gram(0, sub)
    reduce_1(0)
    pump(2)
    reduce_2(0)
    pump(4)
    reduce_3(0)
    pump(4)
    reduce_4(0)
    pump(3)
    reduce_5(0)
    newton(0, lambda: pump(3))
    for sub in range(SUBS):
        apply(0, sub, False)
    own_copy(1).wait()
    for sub in range(SUBS):
        if sub + SUBS + 1 < 2 * SUBS:
            pump((sub + SUBS + 2) * PEERS - sent[0])
        a2a_arrived(1, sub)
        gram(1, sub)
        if sub < SUBS - 1:
            apply(0, sub, True)
    reduce_1(1)
    apply(0, SUBS - 1, True)
    reduce_2(1)
    reduce_3(1)
    reduce_4(1)
    reduce_5(1)
    newton(1, lambda: None)
    for sub in range(SUBS):
        apply(1, sub, False)
    for sub in range(SUBS):
        apply(1, sub, True)

    def a2a_drain(n, carry):
        a2a_copy(n).wait_send()
        return carry

    lax.fori_loop(SENDS - PEERS, SENDS, a2a_drain, 0)
    for stage in range(2):
        for sub in range(SUBS):
            send_copy(stage, sub).wait()
            keep_copy(stage, sub).wait()


def body(samples):
    sems = lambda *shape: pltpu.SemaphoreType.DMA(shape)
    square = (PAIR, PAIR)
    out = pl.pallas_call(
        kernel,
        out_shape=jax.ShapeDtypeStruct((CHIPS, 2, SUBS, CHUNK, PAIR), BF16),
        in_specs=[pl.BlockSpec(memory_space=pl.ANY)],
        out_specs=pl.BlockSpec(memory_space=pl.ANY),
        scratch_shapes=[
            pltpu.VMEM((2, SUBS, CHIPS, CHUNK, PAIR), BF16),
            pltpu.VMEM((2, PACKED, HALF), F32),
            pltpu.VMEM((2, CORE_PART, HALF), F32),
            pltpu.VMEM((2, 3, QUARTER, HALF), F32),
            pltpu.VMEM((2, PACKED, HALF), F32),
            pltpu.VMEM(square, F32), pltpu.VMEM(square, F32),
            *[pltpu.VMEM(square, BF16)] * 6,
            pltpu.VMEM((2, *square), BF16),
            pltpu.VMEM((2, SUBS, CHIPS, CHUNK, HALF), BF16),
            pltpu.VMEM((2, SUBS, CHIPS, CHUNK, HALF), BF16),
            sems(2), sems(PEERS), sems(2 * SUBS), sems(2), sems(2), sems(2, 3), sems(2, 3), sems(2, 3), sems(2, 3),
            sems(2), sems(2), sems(2, SUBS), sems(2, SUBS), sems(2, SUBS),
        ],
        compiler_params=pltpu.CompilerParams(
            collective_id=0, has_side_effects=True, vmem_limit_bytes=56 * 2**20
        ),
    )(samples.reshape(SUBS, CHUNK, samples.shape[1]))
    return out.reshape(-1, PAIR)


def solution(mesh):
    return jax.shard_map(
        body, mesh=mesh, in_specs=(P(("row", "pair"), None),), out_specs=P("row", "pair"), check_vma=False
    )
```

time: 360 us -> 231 us (0.64)
  Pallas kernels: 0 us -> 223 us
  waiting for transfers between devices: 141 us -> 0 us
  blocking collectives: 106 us -> 0 us
  matrix products: 41.7 us -> 0 us
  local copies, waits for them, and re-layouts: 46.4 us -> 7.32 us
  between operations: 14.3 us -> 0.01 us
  other arithmetic: 9.94 us -> 0 us
    pallas_call x0 -> x1, Pallas kernels: none -> 223 us  [body(): pl.pallas_call(kernel, out_shape=jax.ShapeDtypeStruct((CHIPS, 2, SUBS, CH...]
    all_to_all x1 -> x0, blocking collectives: 106 us -> none  [body(): lax.all_to_all(samples, 'pair', split_axis=1, concat_axis=0, tiled=True)]
    ppermute x1 -> x0, waiting for transfers between devices: 96 us -> none  [shifted(): lax.ppermute(shard, axis, [(i, (i + by) % peers) for i in range(peers)])]
    psum x1 -> x0, waiting for transfers between devices: 45.1 us -> none  [body(): gram_matrix = lax.psum(cross_product(relaid, relaid), 'row')]
    dot_general x16 -> x0, matrix products: 41.7 us -> none  [the longest x1 10.2 us: body(): jnp.dot(relaid, rotation, preferred_element_type=jnp.float32)]
    all_to_all x1 -> x0, local copies, waits for them, and re-layouts: 12 us -> none  [body(): lax.all_to_all(samples, 'pair', split_axis=1, concat_axis=0, tiled=True)]
    concatenate x1 -> x0, local copies, waits for them, and re-layouts: 11.9 us -> none  [body(): return jnp.concatenate([turned[:, :middle], moved], axis=1)]
    unnamed x7 -> x1, local copies, waits for them, and re-layouts: 17.3 us -> 7.32 us
  transfers between devices with their start and end apart: 2 -> 0, of which waited for: 2 -> 0; matrix products, arithmetic and copies ran while one was open for 0% -> 0% of each run, Pallas kernels for 0% -> 0%
where the time goes in v1:
time: 231 us
  Pallas kernels  223 us (97%)
  local copies, waits for them, and re-layouts  7.32 us (3%)
    pallas_call x1, Pallas kernels, body(): pl.pallas_call(kernel, out_shape=jax.ShapeDtypeStruct((CHIPS, 2, SUBS, CH...  223 us
    unnamed x1, local copies, waits for them, and re-layouts  7.32 us

profile of v1, /device:TPU:1, one launch (start us, length us, event | category | flops | bytes accessed | tf_op | source)
XLA Modules:
  0.0 230.5 jit_solution(14879668801723159062)
XLA Ops:
  0.0 223.2 %shard_map.17 = bf16[16,2,4,64,512]{4,3,2,1,0:T(8,128)(2,1)} custom-call(bf16[4,64,16384]{2,1,0:T(8,128)(2,1)} %bitcast.3), custom_call_target="tpu_custom_call" | custom-call | tf_op jit(solution)/shard_map/pallas_call | solution.py:337
  223.2 7.3 %copy.3 = bf16[8192,512]{1,0:T(8,128)(2,1)} copy(bf16[8192,512]{1,0:T(8,128)(2,1)} %bitcast.2) | data formatting | bytes 16777216

commit v2 on v1

--- a/solution.py
+++ b/solution.py
@@ -22,6 +22,8 @@
 CORE_PART = PACKED // 2
 QUARTER = CORE_PART // 4
 SENDS = 2 * SUBS * PEERS
+WINDOW = SUBS * PEERS
+SHARED = 2
 
 
 def dot(left, right, dims=((1,), (0,))):
@@ -34,17 +36,19 @@
     ref_lo[...] = (value - high.astype(F32)).astype(BF16)
 
 
-def product(left, right):
+def product(left, right, fine=True):
     lh, ll = left
     rh, rl = right
+    if not fine:
+        return dot(lh[...], rh[...])
     return dot(lh[...], rh[...]) + (dot(lh[...], rl[...]) + dot(ll[...], rh[...]))
 
 
 def kernel(
     x_ref, o_ref,
-    y, part, from_core, from_quarter, full, zmat, mmat, zh, zl, mh, ml, th, tl, rot, w_send, w_keep,
+    y, part, from_core, from_quarter, full, zmat, mmat, zh, zl, mh, ml, th, tl, rot, w_send, w_keep, shared, w_shared,
     own_sem, a2a_send, a2a_recv, core_send, core_recv, rs_send, rs_recv, ag_send, ag_recv,
-    back_send, back_recv, w_send_sem, w_recv_sem, w_keep_sem,
+    back_send, back_recv, w_send_sem, w_recv_sem, w_keep_sem, share_send, share_recv, w_shared_sem,
 ):
     row = lax.axis_index("row")
     pair = lax.axis_index("pair")
@@ -116,7 +120,7 @@
         return pltpu.make_async_remote_copy(
             src_ref=x_ref.at[sub, :, columns_of(stage, target)],
             dst_ref=y.at[stage, sub, chip],
-            send_sem=a2a_send.at[i],
+            send_sem=a2a_send.at[lax.rem(n, WINDOW)],
             recv_sem=a2a_recv.at[phase],
             device_id=(row, target * 2 + plane),
             device_id_type=MESH,
@@ -127,7 +131,7 @@
         return carry
 
     def a2a_next(n, carry):
-        a2a_copy(n - PEERS).wait_send()
+        a2a_copy(n - WINDOW).wait_send()
         a2a_copy(n).start()
         return carry
 
@@ -225,7 +229,7 @@
         lax.broadcasted_iota(jnp.int32, (PAIR, PAIR), 0) == lax.broadcasted_iota(jnp.int32, (PAIR, PAIR), 1)
     ).astype(F32)
 
-    def newton(stage, between):
+    def newton(stage):
         g00 = full[stage, pl.ds(0, HALF)]
         g01 = full[stage, pl.ds(HALF, HALF)]
         g11 = full[stage, pl.ds(2 * HALF, HALF)]
@@ -240,17 +244,16 @@
         mmat[HALF:, HALF:] = g11 / norm
         split(mh, ml, mmat[...])
         zmat[...] = 1.5 * diagonal() - 0.5 * mmat[...]
-        mmat[...] = 1.5 * mmat[...] - 0.5 * product((mh, ml), (mh, ml))
+        mmat[...] = 1.5 * mmat[...] - 0.5 * product((mh, ml), (mh, ml), False)
         split(zh, zl, zmat[...])
         split(mh, ml, mmat[...])
-        between()
-        for _ in range(NS_STEPS - 2):
-            split(th, tl, product((zh, zl), (mh, ml)))
-            mmat[...] = 1.5 * mmat[...] - 0.5 * product((mh, ml), (th, tl))
-            zmat[...] = 1.5 * zmat[...] - 0.5 * product((th, tl), (zh, zl))
+        for step in range(1, NS_STEPS - 1):
+            fine = step >= NS_STEPS - 2
+            split(th, tl, product((zh, zl), (mh, ml), fine))
+            mmat[...] = 1.5 * mmat[...] - 0.5 * product((mh, ml), (th, tl), fine)
+            zmat[...] = 1.5 * zmat[...] - 0.5 * product((th, tl), (zh, zl), fine)
             split(zh, zl, zmat[...])
             split(mh, ml, mmat[...])
-            between()
         split(th, tl, product((zh, zl), (mh, ml)))
         last = 1.5 * zmat[...] - 0.5 * product((th, tl), (zh, zl))
         rot[stage] = (last * jnp.sqrt(ROWS / norm)).astype(BF16)
@@ -274,36 +277,52 @@
             w_keep_sem.at[stage, sub],
         )
 
+    def share_copy(sub):
+        return pltpu.make_async_remote_copy(
+            src_ref=y.at[0, sub], dst_ref=shared.at[sub],
+            send_sem=share_send.at[sub], recv_sem=share_recv.at[sub],
+            device_id=partner(0), device_id_type=MESH,
+        )
+
+    def shared_keep_copy(sub):
+        return pltpu.make_async_copy(
+            w_shared.at[sub],
+            o_ref.at[:, 1 - plane, sub, :, half_of(0, True)],
+            w_shared_sem.at[sub],
+        )
+
+    def apply_shared(sub):
+        share_copy(sub).wait_recv()
+        rows = shared[sub].reshape(CHIPS * CHUNK, PAIR)
+        value = dot(rows, rot[0, :, half_of(0, True)]).astype(BF16)
+        w_shared[sub] = value.reshape(CHIPS, CHUNK, HALF)
+        shared_keep_copy(sub).start()
+
     def apply(stage, sub, kept):
         rows = y[stage, sub].reshape(CHIPS * CHUNK, PAIR)
         value = dot(rows, rot[stage, :, half_of(stage, kept)]).astype(BF16)
         (w_keep if kept else w_send)[stage, sub] = value.reshape(CHIPS, CHUNK, HALF)
         (keep_copy if kept else send_copy)(stage, sub).start()
 
-    lax.fori_loop(0, PEERS, a2a_first, 0)
-    sent[0] = PEERS
+    lax.fori_loop(0, WINDOW, a2a_first, 0)
+    sent[0] = WINDOW
     for sub in range(SUBS):
         pump(PEERS)
         if sub == 0:
             own_copy(0).wait()
         a2a_arrived(0, sub)
+        if sub < SHARED:
+            share_copy(sub).start()
         gram(0, sub)
     reduce_1(0)
-    pump(2)
     reduce_2(0)
-    pump(4)
     reduce_3(0)
-    pump(4)
     reduce_4(0)
-    pump(3)
     reduce_5(0)
-    newton(0, lambda: pump(3))
-    for sub in range(SUBS):
-        apply(0, sub, False)
+    newton(0)
+    apply(0, 2, False)
     own_copy(1).wait()
     for sub in range(SUBS):
-        if sub + SUBS + 1 < 2 * SUBS:
-            pump((sub + SUBS + 2) * PEERS - sent[0])
         a2a_arrived(1, sub)
         gram(1, sub)
         if sub < SUBS - 1:
@@ -311,10 +330,13 @@
     reduce_1(1)
     apply(0, SUBS - 1, True)
     reduce_2(1)
+    apply_shared(0)
     reduce_3(1)
+    apply(0, 3, False)
+    apply_shared(1)
     reduce_4(1)
     reduce_5(1)
-    newton(1, lambda: None)
+    newton(1)
     for sub in range(SUBS):
         apply(1, sub, False)
     for sub in range(SUBS):
@@ -324,11 +346,15 @@
         a2a_copy(n).wait_send()
         return carry
 
-    lax.fori_loop(SENDS - PEERS, SENDS, a2a_drain, 0)
+    lax.fori_loop(SENDS - WINDOW, SENDS, a2a_drain, 0)
     for stage in range(2):
         for sub in range(SUBS):
-            send_copy(stage, sub).wait()
+            if stage == 1 or sub >= SHARED:
+                send_copy(stage, sub).wait()
             keep_copy(stage, sub).wait()
+    for sub in range(SHARED):
+        share_copy(sub).wait_send()
+        shared_keep_copy(sub).wait()
 
 
 def body(samples):
@@ -350,8 +376,11 @@
             pltpu.VMEM((2, *square), BF16),
             pltpu.VMEM((2, SUBS, CHIPS, CHUNK, HALF), BF16),
             pltpu.VMEM((2, SUBS, CHIPS, CHUNK, HALF), BF16),
-            sems(2), sems(PEERS), sems(2 * SUBS), sems(2), sems(2), sems(2, 3), sems(2, 3), sems(2, 3), sems(2, 3),
+            pltpu.VMEM((SHARED, CHIPS, CHUNK, PAIR), BF16),
+            pltpu.VMEM((SHARED, CHIPS, CHUNK, HALF), BF16),
+            sems(2), sems(WINDOW), sems(2 * SUBS), sems(2), sems(2), sems(2, 3), sems(2, 3), sems(2, 3), sems(2, 3),
             sems(2), sems(2), sems(2, SUBS), sems(2, SUBS), sems(2, SUBS),
+            sems(SHARED), sems(SHARED), sems(SHARED),
         ],
         compiler_params=pltpu.CompilerParams(
             collective_id=0, has_side_effects=True, vmem_limit_bytes=56 * 2**20

time: 231 us -> 191 us (0.83)
  Pallas kernels: 223 us -> 183 us
    pallas_call x1, Pallas kernels: 223 us -> 183 us  [body(): pl.pallas_call(kernel, out_shape=jax.ShapeDtypeStruct((CHIPS, 2, SUBS, CH...]
where the time goes in v2:
time: 191 us
  Pallas kernels  183 us (96%)
  local copies, waits for them, and re-layouts  7.32 us (4%)
    pallas_call x1, Pallas kernels, body(): pl.pallas_call(kernel, out_shape=jax.ShapeDtypeStruct((CHIPS, 2, SUBS, CH...  183 us
    unnamed x1, local copies, waits for them, and re-layouts  7.32 us

profile of v2, /device:TPU:1, one launch (start us, length us, event | category | flops | bytes accessed | tf_op | source)
XLA Modules:
  0.0 190.7 jit_solution(3443350541829122252)
XLA Ops:
  0.0 183.4 %shard_map.17 = bf16[16,2,4,64,512]{4,3,2,1,0:T(8,128)(2,1)} custom-call(bf16[4,64,16384]{2,1,0:T(8,128)(2,1)} %bitcast.3), custom_call_target="tpu_custom_call" | custom-call | tf_op jit(solution)/shard_map/pallas_call | solution.py:363
  183.4 7.3 %copy.3 = bf16[8192,512]{1,0:T(8,128)(2,1)} copy(bf16[8192,512]{1,0:T(8,128)(2,1)} %bitcast.2) | data formatting | bytes 16777216

commit v3 on v2

--- a/solution.py
+++ b/solution.py
@@ -248,7 +248,7 @@
         split(zh, zl, zmat[...])
         split(mh, ml, mmat[...])
         for step in range(1, NS_STEPS - 1):
-            fine = step >= NS_STEPS - 2
+            fine = step >= NS_STEPS - 1
             split(th, tl, product((zh, zl), (mh, ml), fine))
             mmat[...] = 1.5 * mmat[...] - 0.5 * product((mh, ml), (th, tl), fine)
             zmat[...] = 1.5 * zmat[...] - 0.5 * product((th, tl), (zh, zl), fine)

time: 191 us -> 188 us (0.984)
  Pallas kernels: 183 us -> 180 us
    pallas_call x1, Pallas kernels: 183 us -> 180 us  [body(): pl.pallas_call(kernel, out_shape=jax.ShapeDtypeStruct((CHIPS, 2, SUBS, CH...]
where the time goes in v3:
time: 188 us
  Pallas kernels  180 us (96%)
  local copies, waits for them, and re-layouts  7.32 us (4%)
    pallas_call x1, Pallas kernels, body(): pl.pallas_call(kernel, out_shape=jax.ShapeDtypeStruct((CHIPS, 2, SUBS, CH...  180 us
    unnamed x1, local copies, waits for them, and re-layouts  7.32 us

profile of v3, /device:TPU:1, one launch (start us, length us, event | category | flops | bytes accessed | tf_op | source)
XLA Modules:
  0.0 187.8 jit_solution(3284448325889055419)
XLA Ops:
  0.0 180.5 %shard_map.17 = bf16[16,2,4,64,512]{4,3,2,1,0:T(8,128)(2,1)} custom-call(bf16[4,64,16384]{2,1,0:T(8,128)(2,1)} %bitcast.3), custom_call_target="tpu_custom_call" | custom-call | tf_op jit(solution)/shard_map/pallas_call | solution.py:363
  180.5 7.3 %copy.3 = bf16[8192,512]{1,0:T(8,128)(2,1)} copy(bf16[8192,512]{1,0:T(8,128)(2,1)} %bitcast.2) | data formatting | bytes 16777216
